TPU v7x, 256 devices: a whole 4x4x8 slice. The times are simulated.
256 devices in a mesh: dp: 16 (over y, z_lo), tensor: 16 (over z_hi, x, core).
Axes of the slice: x: 4, y: 4, z: 8 (z_hi: 2, z_lo: 4; z = z_hi * 4 + z_lo), core: 2. Of those that a mesh axis runs over, the one named last changes fastest.
Arguments:
- activations: bfloat16 [2048, 8192], P('dp', 'tensor'), may hold values from -6 to 6
- out_grads: bfloat16 [2048, 28672], P('dp', 'tensor'), may hold values from -12 to 12
- basis_in: bfloat16 [8192, 8192], P('dp', 'tensor'), may hold values from -0.0625 to 0.0625
- basis_out: bfloat16 [28672, 14336], P('tensor', 'dp'), may hold values from -0.03125 to 0.03125
Outputs:
- correction: float32 [8192, 14336], P('tensor', 'dp')
All inputs are finite; a program needn't handle non-finite values.
Results may differ from a plain program's by a relative error of at most 0.0033.
Values may be sent and summed in bfloat16 or wider, within the bound.
A program may use at most 128 MiB of HBM per device.

v0:
```python
import jax
import jax.numpy as jnp
from jax import lax
from jax.sharding import PartitionSpec as P

SEQ = 128


def local(activations, out_grads, basis_in, basis_out):
    grad_partial = jnp.dot(
        lax.all_gather(out_grads, "dp", axis=0, tiled=True),
        basis_out,
        preferred_element_type=jnp.float32,
    )
    grad_rot = lax.psum(grad_partial, "tensor").astype(jnp.bfloat16)
    full_rows = lax.all_gather(activations, "tensor", axis=1, tiled=True)
    own_rows = jnp.dot(
        full_rows,
        lax.all_gather(basis_in, "dp", axis=0, tiled=True),
        preferred_element_type=jnp.float32,
    ).astype(jnp.bfloat16)
    act_rot = lax.all_gather(own_rows, "dp", axis=0, tiled=True)
    examples = act_rot.shape[0] // SEQ
    per_group = 4
    groups = examples // per_group
    act_groups = act_rot.reshape(groups, per_group, SEQ, act_rot.shape[1])
    grad_groups = grad_rot.reshape(groups, per_group, SEQ, grad_rot.shape[1])

    def accumulate(running, group_pair):
        products = jnp.einsum(
            "nsi,nsj->nij", group_pair[0], group_pair[1], preferred_element_type=jnp.float32
        )
        return (running + jnp.sum(products * products, axis=0), None)

    start_sum = jnp.zeros((act_rot.shape[1], grad_rot.shape[1]), jnp.float32)
    running, unused = lax.scan(accumulate, start_sum, (act_groups, grad_groups))
    return running / (examples * SEQ)


def solution(mesh):
    in_specs = (P("dp", "tensor"), P("dp", "tensor"), P("dp", "tensor"), P("tensor", "dp"))
    out_specs = P("tensor", "dp")
    return jax.shard_map(local, mesh=mesh, in_specs=in_specs, out_specs=out_specs, check_vma=False)
```

profile of v0, /device:TPU:89, one launch (start us, length us, event | category | flops | bytes accessed | tf_op | source)
XLA Modules:
  0.0 671.9 jit_solution(14654089432642550735)
XLA Ops:
  6.5 0.0 copy-start
  6.5 0.0 all-gather.11.cloned.1.call-start
  6.5 0.7 all-gather.11.cloned.1.call-update
  7.3 0.0 all-gather.5.cloned.1.call-start
  7.3 0.7 all-gather.5.cloned.1.call-update
  8.0 0.0 all-gather.7.cloned.1.call-start
  8.1 0.7 all-gather.7.cloned.1.call-update
  8.7 0.0 all-gather.9.cloned.1.call-start
  8.8 163.9 %all-gather.11.cloned.1.call-done = bf16[2048,1792]{1,0:T(8,128)(2,1)} async-done(((bf16[128,1792]{1,0:T(8,128)(2,1)}), bf16[2048,1792]{1,0:T(8,128)(2,1)}) %all-gather.11.cloned.1.call-update) | async-done | bytes 7340048 | tf_op jit(solution)/shard_map/all_gather | solution.py:11
  172.7 0.0 copy-done
  172.7 11.8 %fusion.5 = f32[2048,896]{1,0:T(8,128)} fusion(bf16[2048,1792]{1,0:T(8,128)(2,1)} %all-gather.11.cloned.1.call-done, bf16[1792,896]{1,0:T(8,128)(2,1)S(1)} %copy-done), kind=kOutput, calls=%fused_computation.9 | convolution fusion | flops 6576668672 | bytes 17891328 | tf_op jit(solution)/shard_map/dot_general | solution.py:10
  184.5 53.1 %all-gather.5.cloned.1.call-done = bf16[128,8192]{1,0:T(8,128)(2,1)} async-done(((bf16[128,512]{1,0:T(8,128)(2,1)}), bf16[128,8192]{1,0:T(8,128)(2,1)}) %all-gather.5.cloned.1.call-update) | async-done | bytes 2097168 | tf_op jit(solution)/shard_map/all_gather | solution.py:16
  237.5 183.9 %all-gather.7.cloned.1.call-done = bf16[8192,512]{1,0:T(8,128)(2,1)} async-done(((bf16[512,512]{1,0:T(8,128)(2,1)}), bf16[8192,512]{1,0:T(8,128)(2,1)}) %all-gather.7.cloned.1.call-update) | async-done | bytes 8388624 | tf_op jit(solution)/shard_map/all_gather | solution.py:19
  421.4 5.9 convolution_convert_fusion
  427.4 0.0 all-gather.9.cloned.1.call-update
  427.4 217.1 %all-reduce.1 = bf16[2048,896]{1,0:T(8,128)(2,1)} all-reduce(f32[2048,896]{1,0:T(8,128)} %fusion.5), channel_id=1, replica_groups=mesh['dp'=16,'tensor'=16] {'tensor'}, use_global_device_ids=true, to_apply=%region_0.0 | all-reduce | flops 1835008 | bytes 11010048 | tf_op jit(solution)/shard_map/psum | solution.py:15
  644.5 0.0 all-gather.9.cloned.1.call-done
  644.5 18.1 %while.11 = (s32[]{:T(128)}, f32[512,896]{1,0:T(8,128)}, bf16[4,4,128,512]{3,2,1,0:T(8,128)(2,1)}, bf16[4,4,128,896]{3,2,1,0:T(8,128)(2,1)}, s32[]{:T(128)}, /*index=5*/s32[]{:T(128)}) while((s32[]{:T(128)}, f32[512,896]{1,0:T(8,128)}, bf16[4,4,128,512]{3,2,1,0:T(8,128)(2,1)}, bf16[4,4,128,896]{3,2,1,0:T(8,128)(2,1)}, s32[]{:T(128)}, ...), condition=%wide.region_3.4_spmd.clone, body=%wide.region_1.3_spmd.clone.sunk | while | flops 473890816 | bytes 23463056 | solution.py:36
  644.5 0.0 copy-start.1
  644.5 2.8 multiply_reduce_fusion.2
  647.3 0.0 copy-done.1
  647.3 0.5 select_add_fusion.2
  647.8 0.0 copy-start.2
  647.8 1.2 copy-done.2
  649.0 0.0 copy-start.1
  649.0 2.8 multiply_reduce_fusion.2
  651.8 0.0 copy-done.1
  651.8 0.5 select_add_fusion.2
  652.3 0.0 copy-start.2
  652.3 1.2 copy-done.2
  653.5 0.0 copy-start.1
  653.5 2.8 multiply_reduce_fusion.2
  656.3 0.0 copy-done.1
  656.3 0.5 select_add_fusion.2
  656.8 0.0 copy-start.2
  656.8 1.2 copy-done.2
  658.0 0.0 copy-start.1
  658.0 2.8 multiply_reduce_fusion.2
  660.8 0.0 copy-done.1
  660.8 0.5 select_add_fusion.2
  661.3 0.0 copy-start.2
  661.3 1.2 copy-done.2
  662.6 2.8 broadcast_multiply_fusion
  (1 shorter events, 0.0 us)
Async XLA Ops:
  6.5 166.2 %copy-start = (bf16[1792,896]{1,0:T(8,128)(2,1)S(1)}, bf16[1792,896]{1,0:T(8,128)(2,1)}, u32[]{:S(2)}) copy-start(bf16[1792,896]{1,0:T(8,128)(2,1)} %param.9) | copy-start | bytes 9633796
  6.5 166.2 %all-gather.11.cloned.1.call-start = ((), (), s32[]{:S(2)}) async-start(), calls=%async_computation.3 | async-start | bytes 7798784 | tf_op jit(solution)/shard_map/all_gather | solution.py:11
  7.3 230.3 %all-gather.5.cloned.1.call-start = ((), (), s32[]{:S(2)}) async-start(), calls=%async_computation | async-start | bytes 2228224 | tf_op jit(solution)/shard_map/all_gather | solution.py:16
  8.0 413.4 %all-gather.7.cloned.1.call-start = ((), (), s32[]{:S(2)}) async-start(), calls=%async_computation.1 | async-start | bytes 8912896 | tf_op jit(solution)/shard_map/all_gather | solution.py:19
  8.7 635.7 %all-gather.9.cloned.1.call-start = ((), (), s32[]{:S(2)}) async-start(), calls=%async_computation.2 | async-start | bytes 2228224 | tf_op jit(solution)/shard_map/all_gather | solution.py:22
  644.5 2.8 copy-start.1
  647.8 1.2 copy-start.2
  649.0 2.8 copy-start.1
  652.3 1.2 copy-start.2
  653.5 2.8 copy-start.1
  656.8 1.2 copy-start.2
  658.0 2.8 copy-start.1
  661.3 1.2 copy-start.2
Sparse Core Ops, SparseCore 0:
  9.1 163.4 all-gather.10
  175.2 62.2 all-gather.4
  239.3 182.0 all-gather.6
  427.5 108.7 all-gather.8
where the time goes:
time: 680 us; the launch traced here: 672 us
  waiting for transfers between devices  403 us (59%)
  blocking collectives  217 us (32%)
  matrix products  28.8 us (4%)
  between operations  13.1 us (2%)
    psum x1, blocking collectives, local(): grad_rot = lax.psum(grad_partial, 'tensor').astype(jnp.bfloat16)  217 us
    all_gather x1, waiting for transfers between devices, local(): lax.all_gather(basis_in, 'dp', axis=0, tiled=True)  184 us
    all_gather x1, waiting for transfers between devices, local(): lax.all_gather(out_grads, 'dp', axis=0, tiled=True)  164 us
    all_gather x1, waiting for transfers between devices, local(): full_rows = lax.all_gather(activations, 'tensor', axis=1, tiled=True)  53.1 us
  transfers between devices with their start and end apart: 4, of which 3 were waited for; matrix products, arithmetic and copies ran while one was open for 2% of the time, Pallas kernels for 0%

commit v1 on v0

v1 whole, which is shorter than its diff:
```python
import functools

import jax
import jax.numpy as jnp
from jax import lax
from jax.experimental import pallas as pl
from jax.experimental.pallas import tpu as pltpu
from jax.sharding import PartitionSpec as P

MESH = pl.DeviceIdType.MESH
F32 = jnp.float32
BF16 = jnp.bfloat16
SEQ = 128


class Copies:
    def __init__(self, send_sems):
        self.send_sems = send_sems
        self.sent = []

    def send(self, src, dst, recv_sem, to, cond=None):
        index = len(self.sent)

        def build():
            return pltpu.make_async_remote_copy(
                src_ref=src,
                dst_ref=dst,
                send_sem=self.send_sems.at[index],
                recv_sem=recv_sem,
                device_id=to,
                device_id_type=MESH,
            )

        if cond is None:
            build().start()
        else:
            pl.when(cond)(lambda: build().start())
        self.sent.append((build, cond))

    def finish(self):
        for build, cond in self.sent:
            if cond is None:
                build().wait_send()
            else:
                pl.when(cond)(lambda build=build: build().wait_send())


def kernel(
    tokens_ref, grads_ref, bin_ref, bout_ref, out_ref,
    a_all, part, core_in, x_in, x_sum, z_in, grad, b1, a1, r_part, r_in, rt,
    send_sems, local_sems, a_sem, a_half_sem, b1_sem, b1_half_sem, a1_first_sem, a1_x_sem, a1_core_sem,
    r_sem, rt_z_sem, rt_y_sem, rt_half_sem, core_sem, x_sem, z_sem, gz_sem, gx_sem, gc_sem,
):
    dp, tensor = lax.axis_index("dp"), lax.axis_index("tensor")
    y, zl = dp // 4, dp % 4
    zh, x, c = tensor // 8, (tensor // 2) % 4, tensor % 2

    def dev(x=x, y=y, zl=zl, zh=zh, c=c):
        return (y * 4 + zl, zh * 8 + x * 2 + c)

    def ring(v, k):
        return lax.rem(v + k + 4, 4)

    up_y, down_y = dev(y=ring(y, 1)), dev(y=ring(y, -1))
    core_mate, z_mate = dev(c=1 - c), dev(zh=1 - zh)
    x_others = [dev(x=ring(x, k)) for k in (1, 2, 3)]
    copies = Copies(send_sems)

    barrier = pltpu.get_barrier_semaphore()
    greeted = 0
    for dz in range(4):
        for dh in range(2):
            for dc in range(2):
                if dz or dh or dc:
                    pl.semaphore_signal(
                        barrier, inc=1, device_id=dev(zl=ring(zl, dz), zh=(zh + dh) % 2, c=(c + dc) % 2), device_id_type=MESH
                    )
                    greeted += 1
    for other in [up_y, down_y] + x_others:
        pl.semaphore_signal(barrier, inc=1, device_id=other, device_id_type=MESH)
        greeted += 1
    pl.semaphore_wait(barrier, greeted)

    def got(ref, sem):
        pltpu.make_async_copy(ref, ref, sem).wait()

    def shard(yy, zz):
        return a_all.at[pl.ds(pl.multiple_of((yy * 4 + zz) * SEQ, SEQ), SEQ)]

    def half_shard(yy, zz, half):
        return a_all.at[pl.ds(pl.multiple_of((yy * 4 + zz) * SEQ + half * (SEQ // 2), SEQ // 2), SEQ // 2)]

    def send_shard_y(zz, src, cond=None):
        copies.send(src, shard(y, zz), a_sem.at[1, zz], up_y, cond)
        copies.send(src, shard(y, zz), a_sem.at[2, zz], down_y, cond)

    low, high, opposite = ring(y, -1), ring(y, 1), ring(y, 2)

    def relay_shard_y(zz, cond=None):
        def await_both():
            got(shard(low, zz), a_sem.at[1, zz])
            got(shard(high, zz), a_sem.at[2, zz])

        await_both() if cond is None else pl.when(cond)(await_both)
        copies.send(half_shard(low, zz, 0), half_shard(low, zz, 0), a_half_sem.at[0, zz], up_y, cond)
        copies.send(half_shard(high, zz, 1), half_shard(high, zz, 1), a_half_sem.at[1, zz], down_y, cond)

    def relay_step(k):
        for sign in (-1, 1):
            source = zl + sign * k
            relay_shard_y(jnp.clip(source, 0, 3), jnp.logical_and(source >= 0, source <= 3))

    copies.send(grads_ref, shard(y, zl), a_sem.at[0, zl], dev(zl=jnp.minimum(zl + 1, 3)), zl < 3)
    copies.send(grads_ref, shard(y, zl), a_sem.at[0, zl], dev(zl=jnp.maximum(zl - 1, 0)), zl > 0)

    z_target = 2 * (x % 2) + c
    a1_block = a1.at[zl % 2, 2 * zh + x // 2, zl // 2]
    for h in range(2):
        mine = jnp.logical_and(zl == z_target, zh == h)
        copies.send(
            tokens_ref, a1_block, a1_first_sem.at[zl // 2, zh], dev(zl=z_target, zh=h, c=zl % 2), jnp.logical_not(mine)
        )

        @pl.when(mine)
        def _():
            own = pltpu.make_async_copy(tokens_ref, a1_block, local_sems.at[2])
            own.start()
            own.wait()

    send_shard_y(zl, grads_ref)

    def b1_block(yy):
        return b1.at[pl.ds(pl.multiple_of(yy * 512, 512), 512)]

    def b1_half(yy, half):
        return b1.at[pl.ds(pl.multiple_of(yy * 512 + half * 256, 256), 256)]

    copies.send(bin_ref, b1_block(y), b1_sem.at[0], up_y)
    copies.send(bin_ref, b1_block(y), b1_sem.at[1], down_y)
    own_a = pltpu.make_async_copy(grads_ref, shard(y, zl), local_sems.at[0])
    own_b = pltpu.make_async_copy(bin_ref, b1_block(y), local_sems.at[1])
    own_a.start()
    own_b.start()

    def z_step(k):
        for sign in (-1, 1):
            source = zl + sign * k
            there = jnp.logical_and(source >= 0, source <= 3)
            zz = jnp.clip(source, 0, 3)
            pl.when(there)(lambda zz=zz: got(shard(y, zz), a_sem.at[0, zz]))
            if k < 3:
                onward = zl - sign
                copies.send(
                    shard(y, zz), shard(y, zz), a_sem.at[0, zz], dev(zl=jnp.clip(onward, 0, 3)),
                    jnp.logical_and(there, jnp.logical_and(onward >= 0, onward <= 3)),
                )
            send_shard_y(zz, shard(y, zz), there)

    z_step(1)

    parity = zl // 2
    holds = x % 2 == parity
    for zhalf in range(2):
        for h in range(2):
            mine = jnp.logical_and(c + 2 * zhalf == zl, zh == h)
            pl.when(jnp.logical_and(holds, jnp.logical_not(mine)))(
                lambda zhalf=zhalf, h=h: got(a1.at[c, 2 * h + x // 2, zhalf], a1_first_sem.at[zhalf, h])
            )
    for h in range(2):
        block = a1.at[c, 2 * h + x // 2]
        for other in x_others:
            copies.send(block, block, a1_x_sem.at[2 * h + x // 2], other, holds)

    relay_shard_y(zl)

    got(b1_block(low), b1_sem.at[0])
    copies.send(b1_half(low, 0), b1_half(low, 0), b1_half_sem.at[0], up_y)
    got(b1_block(high), b1_sem.at[1])
    copies.send(b1_half(high, 1), b1_half(high, 1), b1_half_sem.at[1], down_y)

    for kq in range(4):
        pl.when(parity + 2 * (kq % 2) != x)(lambda kq=kq: got(a1.at[c, kq], a1_x_sem.at[kq]))
    copies.send(a1.at[c], a1.at[c], a1_core_sem.at[0], core_mate)

    z_step(2)
    relay_step(1)
    z_step(3)
    own_a.wait()

    half_rows, x_rows, z_rows = 256, 64, 32

    def rotate(g):
        @pl.loop(0, 2)
        def _(m):
            rows = pl.ds(pl.multiple_of(g * 512 + m * 256, 256), 256)
            part[rows, :] = jnp.dot(a_all[rows, :], bout_ref[...], preferred_element_type=F32)

        theirs = part.at[pl.ds(pl.multiple_of(g * 512 + (1 - c) * 256, 256), 256)]
        copies.send(theirs, core_in.at[g], core_sem.at[g], core_mate)

    def sum_core(g):
        got(core_in.at[g], core_sem.at[g])
        base = g * 512 + c * 256
        rows = pl.ds(pl.multiple_of(base, 256), 256)
        part[rows, :] = part[rows, :] + core_in[g]
        for k, other in zip((1, 2, 3), x_others):
            piece = part.at[pl.ds(pl.multiple_of(base + ring(x, k) * x_rows, x_rows), x_rows)]
            copies.send(piece, x_in.at[g, k - 1], x_sem.at[g, k - 1], other)

    def sum_x(g):
        for k in range(3):
            got(x_in.at[g, k], x_sem.at[g, k])
        rows = pl.ds(pl.multiple_of(g * 512 + c * 256 + x * x_rows, x_rows), x_rows)
        x_sum[g] = ((part[rows, :] + x_in[g, 0]) + (x_in[g, 1] + x_in[g, 2])).reshape(2, z_rows, x_sum.shape[3])
        copies.send(x_sum.at[g, 1 - zh], z_in.at[g], z_sem.at[g], z_mate)

    def grad_rows(g, first, count):
        return grad.at[pl.ds(pl.multiple_of(g * 512 + first, count), count)]

    def sum_z(g):
        got(z_in.at[g], z_sem.at[g])
        first = c * 256 + x * x_rows + zh * z_rows
        rows = pl.ds(pl.multiple_of(g * 512 + first, z_rows), z_rows)
        grad[rows, :] = (x_sum[g, zh] + z_in[g]).astype(BF16)
        own = grad_rows(g, first, z_rows)
        copies.send(own, own, gz_sem.at[g], z_mate)

    def spread_x(g):
        got(grad_rows(g, c * 256 + x * x_rows + (1 - zh) * z_rows, z_rows), gz_sem.at[g])
        own = grad_rows(g, c * 256 + x * x_rows, x_rows)
        for k, other in zip((1, 2, 3), x_others):
            copies.send(own, own, gx_sem.at[g, k - 1], other)

    def spread_core(g):
        for k in (1, 2, 3):
            got(grad_rows(g, c * 256 + ring(x, -k) * x_rows, x_rows), gx_sem.at[g, k - 1])
        own = grad_rows(g, c * 256, half_rows)
        copies.send(own, own, gc_sem.at[g], core_mate)

    def fit(g, first):
        got(grad_rows(g, (1 - c) * 256, half_rows), gc_sem.at[g])

        @pl.loop(0, 7)
        def _(j):
            cols = pl.ds(pl.multiple_of(j * 128, 128), 128)
            total = None
            for n in range(4):
                right = grad[pl.ds(pl.multiple_of(g * 512 + n * SEQ, SEQ), SEQ), cols]
                product = jnp.dot(rt[g * 4 + n], right, preferred_element_type=F32)
                square = product * product
                total = square if total is None else total + square
            total = total * (1.0 / 2048)
            out_ref[:, cols] = total if first else out_ref[:, cols] + total

    own_b.wait()
    got(b1_half(opposite, 0), b1_half_sem.at[0])
    got(b1_half(opposite, 1), b1_half_sem.at[1])
    got(a1.at[1 - c], a1_core_sem.at[0])

    @pl.loop(0, 4)
    def _(kq):
        left = a1[:, kq].reshape(512, 512)
        right = b1[pl.ds(pl.multiple_of(kq * 512, 512), 512), :]
        term = jnp.dot(left, right, preferred_element_type=F32)

        @pl.when(kq == 0)
        def _():
            r_part[...] = term.reshape(4, SEQ, 512)

        @pl.when(kq != 0)
        def _():
            r_part[...] += term.reshape(4, SEQ, 512)

    def place(zz):
        return (zz % 2) * 2 + zz // 2

    for k in (1, 2, 3):
        zz = ring(zl, k)
        copies.send(r_part.at[place(zz)], r_in.at[k - 1], r_sem.at[k - 1], dev(zl=zz))

    rotate(y)
    relay_step(2)
    relay_step(3)

    def r_block(yy, zz):
        return rt.at[yy * 4 + zz]

    def r_half(yy, zz, half):
        return rt.at[yy * 4 + zz, pl.ds(half * 256, 256)]

    def send_r_y(zz):
        copies.send(r_block(y, zz), r_block(y, zz), rt_y_sem.at[0, zz], up_y)
        copies.send(r_block(y, zz), r_block(y, zz), rt_y_sem.at[1, zz], down_y)

    for k in range(3):
        got(r_in.at[k], r_sem.at[k])
    own_r = (r_part[place(zl)] + r_in[0]) + (r_in[1] + r_in[2])
    rt[y * 4 + zl] = own_r.T.astype(BF16)
    for k in (1, 2, 3):
        copies.send(r_block(y, zl), r_block(y, zl), rt_z_sem.at[k - 1], dev(zl=ring(zl, k)))
    send_r_y(zl)
    sum_core(y)

    for k in (1, 2, 3):
        zz = ring(zl, -k)
        got(r_block(y, zz), rt_z_sem.at[k - 1])
        send_r_y(zz)
    sum_x(y)

    def await_group(yy, which):
        for k in range(4):
            if which == 3:
                got(half_shard(yy, k, 0), a_half_sem.at[0, k])
                got(half_shard(yy, k, 1), a_half_sem.at[1, k])

    rotate(high)
    sum_z(y)
    rotate(low)
    spread_x(y)
    sum_core(high)
    sum_core(low)
    spread_core(y)

    for k in range(4):
        zz = ring(zl, k)
        got(r_block(low, zz), rt_y_sem.at[0, zz])
        copies.send(r_half(low, zz, 0), r_half(low, zz, 0), rt_half_sem.at[0, zz], up_y)
        got(r_block(high, zz), rt_y_sem.at[1, zz])
        copies.send(r_half(high, zz, 1), r_half(high, zz, 1), rt_half_sem.at[1, zz], down_y)

    sum_x(high)
    sum_x(low)
    await_group(opposite, 3)
    rotate(opposite)
    sum_z(high)
    sum_z(low)
    sum_core(opposite)
    spread_x(high)
    spread_x(low)
    fit(y, True)
    sum_x(opposite)
    spread_core(high)
    spread_core(low)
    sum_z(opposite)
    fit(high, False)
    spread_x(opposite)
    fit(low, False)
    spread_core(opposite)
    for k in range(4):
        got(r_half(opposite, k, 0), rt_half_sem.at[0, k])
        got(r_half(opposite, k, 1), rt_half_sem.at[1, k])
    fit(opposite, False)
    copies.finish()


def local(activations, out_grads, basis_in, basis_out):
    vmem = pl.BlockSpec(memory_space=pltpu.VMEM)
    dma = pltpu.SemaphoreType.DMA
    return pl.pallas_call(
        kernel,
        out_shape=jax.ShapeDtypeStruct((512, 896), F32),
        in_specs=[vmem] * 4,
        out_specs=vmem,
        scratch_shapes=[
            pltpu.VMEM((2048, 1792), BF16),
            pltpu.VMEM((2048, 896), F32),
            pltpu.VMEM((4, 256, 896), F32),
            pltpu.VMEM((4, 3, 64, 896), F32),
            pltpu.VMEM((4, 2, 32, 896), F32),
            pltpu.VMEM((4, 32, 896), F32),
            pltpu.VMEM((2048, 896), BF16),
            pltpu.VMEM((2048, 512), BF16),
            pltpu.VMEM((2, 4, 2, 128, 512), BF16),
            pltpu.VMEM((4, 128, 512), F32),
            pltpu.VMEM((3, 128, 512), F32),
            pltpu.VMEM((16, 512, 128), BF16),
            dma((160,)),
            dma((3,)),
            dma((3, 4)),
            dma((2, 4)),
            dma((2,)),
            dma((2,)),
            dma((2, 2)),
            dma((4,)),
            dma((1,)),
            dma((3,)),
            dma((3,)),
            dma((2, 4)),
            dma((2, 4)),
            dma((4,)),
            dma((4, 3)),
            dma((4,)),
            dma((4,)),
            dma((4, 3)),
            dma((4,)),
        ],
        compiler_params=pltpu.CompilerParams(
            collective_id=0, has_side_effects=True, vmem_limit_bytes=56 * 2**20
        ),
        cost_estimate=pl.CostEstimate(flops=9_600_000_000, bytes_accessed=6_000_000, transcendentals=0),
    )(activations, out_grads, basis_in, basis_out)


def solution(mesh):
    in_specs = (P("dp", "tensor"), P("dp", "tensor"), P("dp", "tensor"), P("tensor", "dp"))
    out_specs = P("tensor", "dp")
    return jax.shard_map(local, mesh=mesh, in_specs=in_specs, out_specs=out_specs, check_vma=False)
```

time: 680 us -> 192 us (0.28); the launches traced: 672 us -> 192 us
  waiting for transfers between devices: 403 us -> 0 us
  blocking collectives: 217 us -> 0 us
  Pallas kernels: 0 us -> 189 us
  matrix products: 28.8 us -> 0 us
  between operations: 13.1 us -> 0.01 us
    all_gather x4 -> x0, waiting for transfers between devices: 401 us -> none  [the longest x1 184 us: local(): lax.all_gather(basis_in, 'dp', axis=0, tiled=True)]
    psum x1 -> x0, blocking collectives: 217 us -> none  [local(): grad_rot = lax.psum(grad_partial, 'tensor').astype(jnp.bfloat16)]
    pallas_call x0 -> x1, Pallas kernels: none -> 189 us  [local(): pl.pallas_call(kernel, out_shape=jax.ShapeDtypeStruct((512, 896), F32), i...]
    dot_general x6 -> x0, matrix products: 28.8 us -> none  [the longest x1 11.8 us: local(): jnp.dot(lax.all_gather(out_grads, 'dp', axis=0, tiled=True), basis_out, p...]
  transfers between devices with their start and end apart: 4 -> 0, of which waited for: 3 -> 0; matrix products, arithmetic and copies ran while one was open for 2% -> 0% of each run, Pallas kernels for 0% -> 0%
where the time goes in v1:
time: 192 us
  Pallas kernels  189 us (98%)
  local copies, waits for them, and re-layouts  2.85 us (1%)
    pallas_call x1, Pallas kernels, local(): pl.pallas_call(kernel, out_shape=jax.ShapeDtypeStruct((512, 896), F32), i...  189 us

profile of v1, /device:TPU:89, one launch (start us, length us, event | category | flops | bytes accessed | tf_op | source)
XLA Modules:
  0.0 192.3 jit_solution(11366141601075370085)
XLA Ops:
  0.0 189.5 %shard_map.46 = f32[512,896]{1,0:T(8,128)} custom-call(bf16[128,512]{1,0:T(8,128)(2,1)} %tokens_ref.1, bf16[128,1792]{1,0:T(8,128)(2,1)} %grads_ref.1, bf16[512,512]{1,0:T(8,128)(2,1)} %bin_ref.1, bf16[1792,896]{1,0:T(8,128)(2,1)} %bout_ref.1), custom_call_target="tpu_custom_call" | custom-call | flops 9600000000 | bytes 6000000 | tf_op jit(solution)/shard_map/pallas_call | solution.py:359
  189.5 2.8 %copy.6 = f32[512,896]{1,0:T(8,128)} copy(f32[512,896]{1,0:T(8,128)} %shard_map.46) | data formatting | bytes 3670016

commit v2 on v1

v2 whole, which is shorter than its diff:
```python
import functools

import jax
import jax.numpy as jnp
from jax import lax
from jax.experimental import pallas as pl
from jax.experimental.pallas import tpu as pltpu
from jax.sharding import PartitionSpec as P

MESH = pl.DeviceIdType.MESH
F32 = jnp.float32
BF16 = jnp.bfloat16
SEQ = 128


class Copies:
    def __init__(self, send_sems):
        self.send_sems = send_sems
        self.sent = []

    def send(self, src, dst, recv_sem, to, cond=None):
        index = len(self.sent)

        def build():
            return pltpu.make_async_remote_copy(
                src_ref=src,
                dst_ref=dst,
                send_sem=self.send_sems.at[index],
                recv_sem=recv_sem,
                device_id=to,
                device_id_type=MESH,
            )

        if cond is None:
            build().start()
        else:
            pl.when(cond)(lambda: build().start())
        self.sent.append((build, cond))

    def finish(self):
        for build, cond in self.sent:
            if cond is None:
                build().wait_send()
            else:
                pl.when(cond)(lambda build=build: build().wait_send())


def kernel(
    x_type, r_type,
    tokens_ref, grads_ref, bin_ref, bout_ref, out_ref,
    a_all, part, core_in, x_out, x_in, x_sum, z_in, grad, b1, a1, r_part, r_out, r_in, rt,
    send_sems, local_sems, a_sem, a_half_sem, b1_sem, b1_half_sem, a1_first_sem, a1_x_sem, a1_core_sem,
    r_sem, rt_z_sem, rt_y_sem, rt_half_sem, core_sem, x_sem, z_sem, gz_sem, gx_sem, gc_sem,
):
    dp, tensor = lax.axis_index("dp"), lax.axis_index("tensor")
    y, zl = dp // 4, dp % 4
    zh, x, c = tensor // 8, (tensor // 2) % 4, tensor % 2

    def dev(x=x, y=y, zl=zl, zh=zh, c=c):
        return (y * 4 + zl, zh * 8 + x * 2 + c)

    def ring(v, k):
        return lax.rem(v + k + 4, 4)

    up_y, down_y = dev(y=ring(y, 1)), dev(y=ring(y, -1))
    core_mate, z_mate = dev(c=1 - c), dev(zh=1 - zh)
    x_others = [dev(x=ring(x, k)) for k in (1, 2, 3)]
    copies = Copies(send_sems)

    barrier = pltpu.get_barrier_semaphore()
    greeted = 0
    for dz in range(4):
        for dh in range(2):
            for dc in range(2):
                if dz or dh or dc:
                    pl.semaphore_signal(
                        barrier, inc=1, device_id=dev(zl=ring(zl, dz), zh=(zh + dh) % 2, c=(c + dc) % 2), device_id_type=MESH
                    )
                    greeted += 1
    for other in [up_y, down_y] + x_others:
        pl.semaphore_signal(barrier, inc=1, device_id=other, device_id_type=MESH)
        greeted += 1
    pl.semaphore_wait(barrier, greeted)

    def got(ref, sem):
        pltpu.make_async_copy(ref, ref, sem).wait()

    def shard(yy, zz):
        return a_all.at[pl.ds(pl.multiple_of((yy * 4 + zz) * SEQ, SEQ), SEQ)]

    def half_shard(yy, zz, half):
        return a_all.at[pl.ds(pl.multiple_of((yy * 4 + zz) * SEQ + half * (SEQ // 2), SEQ // 2), SEQ // 2)]

    def send_shard_y(zz, src, cond=None):
        copies.send(src, shard(y, zz), a_sem.at[1, zz], up_y, cond)
        copies.send(src, shard(y, zz), a_sem.at[2, zz], down_y, cond)

    low, high, opposite = ring(y, -1), ring(y, 1), ring(y, 2)

    def relay_shard_y(zz):
        got(shard(low, zz), a_sem.at[1, zz])
        copies.send(half_shard(low, zz, 0), half_shard(low, zz, 0), a_half_sem.at[0, zz], up_y)
        got(shard(high, zz), a_sem.at[2, zz])
        copies.send(half_shard(high, zz, 1), half_shard(high, zz, 1), a_half_sem.at[1, zz], down_y)

    z_target = 2 * (x % 2) + c
    a1_block = a1.at[zl % 2, 2 * zh + x // 2, zl // 2]
    for h in range(2):
        mine = jnp.logical_and(zl == z_target, zh == h)
        copies.send(
            tokens_ref, a1_block, a1_first_sem.at[zl // 2, zh], dev(zl=z_target, zh=h, c=zl % 2), jnp.logical_not(mine)
        )

        @pl.when(mine)
        def _():
            own = pltpu.make_async_copy(tokens_ref, a1_block, local_sems.at[2])
            own.start()
            own.wait()

    def b1_block(yy):
        return b1.at[pl.ds(pl.multiple_of(yy * 512, 512), 512)]

    def b1_half(yy, half):
        return b1.at[pl.ds(pl.multiple_of(yy * 512 + half * 256, 256), 256)]

    copies.send(bin_ref, b1_block(y), b1_sem.at[0], up_y)
    copies.send(bin_ref, b1_block(y), b1_sem.at[1], down_y)
    copies.send(grads_ref, shard(y, zl), a_sem.at[0, zl], dev(zl=jnp.minimum(zl + 1, 3)), zl < 3)
    copies.send(grads_ref, shard(y, zl), a_sem.at[0, zl], dev(zl=jnp.maximum(zl - 1, 0)), zl > 0)

    own_a = pltpu.make_async_copy(grads_ref, shard(y, zl), local_sems.at[0])
    own_b = pltpu.make_async_copy(bin_ref, b1_block(y), local_sems.at[1])
    own_a.start()
    own_b.start()

    def z_step(k):
        for sign in (-1, 1):
            source = zl + sign * k
            there = jnp.logical_and(source >= 0, source <= 3)
            zz = jnp.clip(source, 0, 3)
            pl.when(there)(lambda zz=zz: got(shard(y, zz), a_sem.at[0, zz]))
            if k < 3:
                onward = zl - sign
                copies.send(
                    shard(y, zz), shard(y, zz), a_sem.at[0, zz], dev(zl=jnp.clip(onward, 0, 3)),
                    jnp.logical_and(there, jnp.logical_and(onward >= 0, onward <= 3)),
                )
            send_shard_y(zz, shard(y, zz), there)

    parity = zl // 2

    def tokens_x():
        holds = x % 2 == parity
        for zhalf in range(2):
            for h in range(2):
                mine = jnp.logical_and(c + 2 * zhalf == zl, zh == h)
                pl.when(jnp.logical_and(holds, jnp.logical_not(mine)))(
                    lambda zhalf=zhalf, h=h: got(a1.at[c, 2 * h + x // 2, zhalf], a1_first_sem.at[zhalf, h])
                )
        for h in range(2):
            block = a1.at[c, 2 * h + x // 2]
            for other in x_others:
                copies.send(block, block, a1_x_sem.at[2 * h + x // 2], other, holds)

    def tokens_core():
        for kq in range(4):
            pl.when(parity + 2 * (kq % 2) != x)(lambda kq=kq: got(a1.at[c, kq], a1_x_sem.at[kq]))
        copies.send(a1.at[c], a1.at[c], a1_core_sem.at[0], core_mate)

    def basis_relay():
        got(b1_block(low), b1_sem.at[0])
        copies.send(b1_half(low, 0), b1_half(low, 0), b1_half_sem.at[0], up_y)
        got(b1_block(high), b1_sem.at[1])
        copies.send(b1_half(high, 1), b1_half(high, 1), b1_half_sem.at[1], down_y)

    near, far = zl // 2, 1 - zl // 2
    units = [(y, near), (y, far), (high, near), (low, near), (high, far), (low, far), (opposite, near), (opposite, far)]

    def rotate(i):
        g, h = units[i]
        rows = pl.ds(pl.multiple_of(g * 512 + h * 256, 256), 256)
        part[i] = jnp.dot(a_all[rows, :], bout_ref[...], preferred_element_type=F32)
        theirs = part.at[i, pl.ds(pl.multiple_of((1 - c) * 128, 128), 128)]
        copies.send(theirs, core_in.at[i], core_sem.at[i], core_mate)

    def sum_core(i):
        got(core_in.at[i], core_sem.at[i])
        rows = pl.ds(pl.multiple_of(c * 128, 128), 128)
        chip = part[i, rows, :] + core_in[i]
        part[i, rows, :] = chip
        if x_type == F32:
            for k, other in zip((1, 2, 3), x_others):
                piece = part.at[i, pl.ds(pl.multiple_of(c * 128 + ring(x, k) * 32, 32), 32)]
                copies.send(piece, x_in.at[i, k - 1], x_sem.at[i, k - 1], other)
        else:
            x_out[i] = chip.astype(x_type).reshape(4, 32, chip.shape[1])
            for k, other in zip((1, 2, 3), x_others):
                copies.send(x_out.at[i, ring(x, k)], x_in.at[i, k - 1], x_sem.at[i, k - 1], other)

    def sum_x(i):
        for k in range(3):
            got(x_in.at[i, k], x_sem.at[i, k])
        rows = pl.ds(pl.multiple_of(c * 128 + x * 32, 32), 32)
        others = [x_in[i, k].astype(F32) for k in range(3)]
        x_sum[i] = ((part[i, rows, :] + others[0]) + (others[1] + others[2])).reshape(2, 16, part.shape[2])
        copies.send(x_sum.at[i, 1 - zh], z_in.at[i], z_sem.at[i], z_mate)

    def grad_rows(i, first, count):
        return grad.at[i, pl.ds(pl.multiple_of(first, count), count)]

    def sum_z(i):
        got(z_in.at[i], z_sem.at[i])
        first = c * 128 + x * 32 + zh * 16
        grad[i, pl.ds(pl.multiple_of(first, 16), 16), :] = (x_sum[i, zh] + z_in[i]).astype(BF16)
        own = grad_rows(i, first, 16)
        copies.send(own, own, gz_sem.at[i], z_mate)

    def spread_x(i):
        got(grad_rows(i, c * 128 + x * 32 + (1 - zh) * 16, 16), gz_sem.at[i])
        own = grad_rows(i, c * 128 + x * 32, 32)
        for k, other in zip((1, 2, 3), x_others):
            copies.send(own, own, gx_sem.at[i, k - 1], other)

    def spread_core(i):
        for k in (1, 2, 3):
            got(grad_rows(i, c * 128 + ring(x, -k) * 32, 32), gx_sem.at[i, k - 1])
        own = grad_rows(i, c * 128, 128)
        copies.send(own, own, gc_sem.at[i], core_mate)

    def fit(i):
        got(grad_rows(i, (1 - c) * 128, 128), gc_sem.at[i])
        g, h = units[i]

        @pl.loop(0, 7)
        def _(j):
            cols = pl.ds(pl.multiple_of(j * 128, 128), 128)
            total = None
            for n in range(2):
                right = grad[i, n * SEQ:(n + 1) * SEQ, cols]
                product = jnp.dot(rt[g * 4 + h * 2 + n], right, preferred_element_type=F32)
                square = product * product
                total = square if total is None else total + square
            total = total * (1.0 / 2048)
            out_ref[:, cols] = total if i == 0 else out_ref[:, cols] + total

    def place(zz):
        return (zz % 2) * 2 + zz // 2

    def rotate_act():
        own_b.wait()
        got(b1_half(opposite, 0), b1_half_sem.at[0])
        got(b1_half(opposite, 1), b1_half_sem.at[1])
        got(a1.at[1 - c], a1_core_sem.at[0])

        @pl.loop(0, 4)
        def _(kq):
            left = a1[:, kq].reshape(512, 512)
            right = b1[pl.ds(pl.multiple_of(kq * 512, 512), 512), :]
            term = jnp.dot(left, right, preferred_element_type=F32)

            @pl.when(kq == 0)
            def _():
                r_part[...] = term.reshape(4, SEQ, 512)

            @pl.when(kq != 0)
            def _():
                r_part[...] += term.reshape(4, SEQ, 512)

        source = r_part
        if r_type != F32:
            r_out[...] = r_part[...].astype(r_type)
            source = r_out
        for k in (1, 2, 3):
            zz = ring(zl, k)
            copies.send(source.at[place(zz)], r_in.at[k - 1], r_sem.at[k - 1], dev(zl=zz))

    def r_block(yy, zz):
        return rt.at[yy * 4 + zz]

    def r_half(yy, zz, half):
        return rt.at[yy * 4 + zz, pl.ds(half * 256, 256)]

    def send_r_y(zz):
        copies.send(r_block(y, zz), r_block(y, zz), rt_y_sem.at[0, zz], up_y)
        copies.send(r_block(y, zz), r_block(y, zz), rt_y_sem.at[1, zz], down_y)

    def sum_act():
        for k in range(3):
            got(r_in.at[k], r_sem.at[k])
        others = [r_in[k].astype(F32) for k in range(3)]
        own_r = (r_part[place(zl)] + others[0]) + (others[1] + others[2])
        rt[y * 4 + zl] = own_r.T.astype(BF16)
        for k in (1, 2, 3):
            copies.send(r_block(y, zl), r_block(y, zl), rt_z_sem.at[k - 1], dev(zl=ring(zl, k)))
        send_r_y(zl)

    def act_y(k):
        zz = ring(zl, -k)
        got(r_block(y, zz), rt_z_sem.at[k - 1])
        send_r_y(zz)

    def act_relay(k):
        zz = ring(zl, -k)
        got(r_block(low, zz), rt_y_sem.at[0, zz])
        copies.send(r_half(low, zz, 0), r_half(low, zz, 0), rt_half_sem.at[0, zz], up_y)
        got(r_block(high, zz), rt_y_sem.at[1, zz])
        copies.send(r_half(high, zz, 1), r_half(high, zz, 1), rt_half_sem.at[1, zz], down_y)

    def act_opposite():
        for k in range(4):
            got(r_half(opposite, k, 0), rt_half_sem.at[0, k])
            got(r_half(opposite, k, 1), rt_half_sem.at[1, k])

    def opposite_pair(h):
        for k in range(2):
            got(half_shard(opposite, 2 * h + k, 0), a_half_sem.at[0, 2 * h + k])
            got(half_shard(opposite, 2 * h + k, 1), a_half_sem.at[1, 2 * h + k])

    mate = zl + 1 - 2 * (zl % 2)

    def relay_far():
        relay_shard_y(2 * far)
        relay_shard_y(2 * far + 1)

    stages = [rotate, sum_core, sum_x, sum_z, spread_x, spread_core]

    def slot(s):
        for stage in reversed(range(len(stages))):
            if 0 <= s - stage < 8:
                stages[stage](s - stage)

    tokens_x()
    basis_relay()
    send_shard_y(zl, grads_ref)
    z_step(1)
    own_a.wait()
    slot(0)
    tokens_core()
    z_step(2)
    relay_shard_y(zl)
    rotate_act()
    z_step(3)
    slot(1)
    relay_shard_y(mate)
    slot(2)
    slot(3)
    sum_act()
    relay_far()
    slot(4)
    act_y(1)
    slot(5)
    act_y(2)
    act_y(3)
    opposite_pair(near)
    slot(6)
    fit(0)
    for k in range(4):
        act_relay(k)
    opposite_pair(far)
    slot(7)
    fit(1)
    slot(8)
    fit(2)
    slot(9)
    fit(3)
    slot(10)
    fit(4)
    slot(11)
    fit(5)
    slot(12)
    act_opposite()
    fit(6)
    fit(7)
    copies.finish()


def call(arrays, x_type, r_type, collective_id):
    vmem = pl.BlockSpec(memory_space=pltpu.VMEM)
    dma = pltpu.SemaphoreType.DMA
    return pl.pallas_call(
        functools.partial(kernel, x_type, r_type),
        out_shape=jax.ShapeDtypeStruct((512, 896), F32),
        in_specs=[vmem] * 4,
        out_specs=vmem,
        scratch_shapes=[
            pltpu.VMEM((2048, 1792), BF16),
            pltpu.VMEM((8, 256, 896), F32),
            pltpu.VMEM((8, 128, 896), F32),
            pltpu.VMEM((8, 4, 32, 896), BF16),
            pltpu.VMEM((8, 3, 32, 896), x_type),
            pltpu.VMEM((8, 2, 16, 896), F32),
            pltpu.VMEM((8, 16, 896), F32),
            pltpu.VMEM((8, 256, 896), BF16),
            pltpu.VMEM((2048, 512), BF16),
            pltpu.VMEM((2, 4, 2, 128, 512), BF16),
            pltpu.VMEM((4, 128, 512), F32),
            pltpu.VMEM((4, 128, 512), BF16),
            pltpu.VMEM((3, 128, 512), r_type),
            pltpu.VMEM((16, 512, 128), BF16),
            dma((200,)),
            dma((3,)),
            dma((3, 4)),
            dma((2, 4)),
            dma((2,)),
            dma((2,)),
            dma((2, 2)),
            dma((4,)),
            dma((1,)),
            dma((3,)),
            dma((3,)),
            dma((2, 4)),
            dma((2, 4)),
            dma((8,)),
            dma((8, 3)),
            dma((8,)),
            dma((8,)),
            dma((8, 3)),
            dma((8,)),
        ],
        compiler_params=pltpu.CompilerParams(
            collective_id=collective_id, has_side_effects=True, vmem_limit_bytes=56 * 2**20
        ),
        cost_estimate=pl.CostEstimate(flops=9_600_000_000, bytes_accessed=6_000_000, transcendentals=0),
    )(*arrays)


def solution(mesh):
    in_specs = (P("dp", "tensor"), P("dp", "tensor"), P("dp", "tensor"), P("tensor", "dp"))
    out_specs = P("tensor", "dp")

    def local(*arrays):
        return call(arrays, F32, BF16, 0)

    return jax.shard_map(local, mesh=mesh, in_specs=in_specs, out_specs=out_specs, check_vma=False)
```

time: 192 us -> 154 us (0.80)
  the two profiles are of different devices: /device:TPU:89 before, /device:TPU:1 now
where the time goes in v2:
time: 154 us
  Pallas kernels  151 us (98%)
  local copies, waits for them, and re-layouts  2.85 us (2%)
    pallas_call x1, Pallas kernels, call(): pl.pallas_call(functools.partial(kernel, x_type, r_type), out_shape=jax.S...  151 us

profile of v2, /device:TPU:1, one launch (start us, length us, event | category | flops | bytes accessed | tf_op | source)
XLA Modules:
  0.0 154.1 jit_solution(10719563302522042118)
XLA Ops:
  0.0 151.2 %shard_map.46 = f32[512,896]{1,0:T(8,128)} custom-call(bf16[128,512]{1,0:T(8,128)(2,1)} %tokens_ref.1, bf16[128,1792]{1,0:T(8,128)(2,1)} %grads_ref.1, bf16[512,512]{1,0:T(8,128)(2,1)} %bin_ref.1, bf16[1792,896]{1,0:T(8,128)(2,1)} %bout_ref.1), custom_call_target="tpu_custom_call" | custom-call | flops 9600000000 | bytes 6000000 | tf_op jit(solution)/shard_map/pallas_call | solution.py:380
  151.2 2.8 %copy.6 = f32[512,896]{1,0:T(8,128)} copy(f32[512,896]{1,0:T(8,128)} %shard_map.46) | data formatting | bytes 3670016

commit v3 on v2

--- a/solution.py
+++ b/solution.py
@@ -18,14 +18,14 @@
         self.send_sems = send_sems
         self.sent = []
 
-    def send(self, src, dst, recv_sem, to, cond=None):
+    def send(self, src, dst, recv_sem, to, cond=None, shared=None):
         index = len(self.sent)
 
         def build():
             return pltpu.make_async_remote_copy(
                 src_ref=src,
                 dst_ref=dst,
-                send_sem=self.send_sems.at[index],
+                send_sem=self.send_sems.at[index] if shared is None else shared,
                 recv_sem=recv_sem,
                 device_id=to,
                 device_id_type=MESH,
@@ -35,7 +35,8 @@
             build().start()
         else:
             pl.when(cond)(lambda: build().start())
-        self.sent.append((build, cond))
+        if shared is None:
+            self.sent.append((build, cond))
 
     def finish(self):
         for build, cond in self.sent:
@@ -46,11 +47,11 @@
 
 
 def kernel(
-    x_type, r_type,
+    r_type,
     tokens_ref, grads_ref, bin_ref, bout_ref, out_ref,
-    a_all, part, core_in, x_out, x_in, x_sum, z_in, grad, b1, a1, r_part, r_out, r_in, rt,
+    a_all, part, core_in, x_in, x_sum, z_in, grad, b1, a1, r_part, r_out, r_in, rt,
     send_sems, local_sems, a_sem, a_half_sem, b1_sem, b1_half_sem, a1_first_sem, a1_x_sem, a1_core_sem,
-    r_sem, rt_z_sem, rt_y_sem, rt_half_sem, core_sem, x_sem, z_sem, gz_sem, gx_sem, gc_sem,
+    r_sem, r_send_sem, rt_z_sem, rt_y_sem, rt_y_send_sem, rt_half_sem, core_sem, x_sem, x_send_sem, z_sem, gx_sem, gx_send_sem, gc_sem,
 ):
     dp, tensor = lax.axis_index("dp"), lax.axis_index("tensor")
     y, zl = dp // 4, dp % 4
@@ -188,60 +189,54 @@
         rows = pl.ds(pl.multiple_of(c * 128, 128), 128)
         chip = part[i, rows, :] + core_in[i]
         part[i, rows, :] = chip
-        if x_type == F32:
-            for k, other in zip((1, 2, 3), x_others):
-                piece = part.at[i, pl.ds(pl.multiple_of(c * 128 + ring(x, k) * 32, 32), 32)]
-                copies.send(piece, x_in.at[i, k - 1], x_sem.at[i, k - 1], other)
-        else:
-            x_out[i] = chip.astype(x_type).reshape(4, 32, chip.shape[1])
-            for k, other in zip((1, 2, 3), x_others):
-                copies.send(x_out.at[i, ring(x, k)], x_in.at[i, k - 1], x_sem.at[i, k - 1], other)
+        for k, other in zip((1, 2, 3), x_others):
+            piece = part.at[i, pl.ds(pl.multiple_of(c * 128 + ring(x, k) * 32, 32), 32)]
+            copies.send(piece, x_in.at[i, k - 1], x_sem.at[i], other, shared=x_send_sem.at[i])
 
     def sum_x(i):
-        for k in range(3):
-            got(x_in.at[i, k], x_sem.at[i, k])
+        got(x_in.at[i], x_sem.at[i])
         rows = pl.ds(pl.multiple_of(c * 128 + x * 32, 32), 32)
-        others = [x_in[i, k].astype(F32) for k in range(3)]
-        x_sum[i] = ((part[i, rows, :] + others[0]) + (others[1] + others[2])).reshape(2, 16, part.shape[2])
-        copies.send(x_sum.at[i, 1 - zh], z_in.at[i], z_sem.at[i], z_mate)
+        x_sum[i] = (part[i, rows, :] + x_in[i, 0]) + (x_in[i, 1] + x_in[i, 2])
+        copies.send(x_sum.at[i], z_in.at[i], z_sem.at[i], z_mate)
 
     def grad_rows(i, first, count):
         return grad.at[i, pl.ds(pl.multiple_of(first, count), count)]
 
     def sum_z(i):
         got(z_in.at[i], z_sem.at[i])
-        first = c * 128 + x * 32 + zh * 16
-        grad[i, pl.ds(pl.multiple_of(first, 16), 16), :] = (x_sum[i, zh] + z_in[i]).astype(BF16)
-        own = grad_rows(i, first, 16)
-        copies.send(own, own, gz_sem.at[i], z_mate)
-
-    def spread_x(i):
-        got(grad_rows(i, c * 128 + x * 32 + (1 - zh) * 16, 16), gz_sem.at[i])
-        own = grad_rows(i, c * 128 + x * 32, 32)
-        for k, other in zip((1, 2, 3), x_others):
-            copies.send(own, own, gx_sem.at[i, k - 1], other)
+        first = c * 128 + x * 32
+        grad[i, pl.ds(pl.multiple_of(first, 32), 32), :] = (x_sum[i] + z_in[i]).astype(BF16)
+        own = grad_rows(i, first, 32)
+        for other in x_others:
+            copies.send(own, own, gx_sem.at[i], other, shared=gx_send_sem.at[i])
 
     def spread_core(i):
-        for k in (1, 2, 3):
-            got(grad_rows(i, c * 128 + ring(x, -k) * 32, 32), gx_sem.at[i, k - 1])
+        got(grad.at[i, pl.ds(0, 96)], gx_sem.at[i])
         own = grad_rows(i, c * 128, 128)
         copies.send(own, own, gc_sem.at[i], core_mate)
 
-    def fit(i):
-        got(grad_rows(i, (1 - c) * 128, 128), gc_sem.at[i])
-        g, h = units[i]
-
-        @pl.loop(0, 7)
-        def _(j):
-            cols = pl.ds(pl.multiple_of(j * 128, 128), 128)
+    def fit(pair):
+        examples = []
+        for i in (2 * pair, 2 * pair + 1):
+            got(grad_rows(i, (1 - c) * 128, 128), gc_sem.at[i])
+            g, h = units[i]
+            examples += [(g * 4 + h * 2 + n, i, n * SEQ) for n in range(2)]
+
+        def tile(cols):
             total = None
-            for n in range(2):
-                right = grad[i, n * SEQ:(n + 1) * SEQ, cols]
-                product = jnp.dot(rt[g * 4 + h * 2 + n], right, preferred_element_type=F32)
+            for example, i, first in examples:
+                right = grad[i, first:first + SEQ, cols]
+                product = jnp.dot(rt[example], right, preferred_element_type=F32)
                 square = product * product
                 total = square if total is None else total + square
             total = total * (1.0 / 2048)
-            out_ref[:, cols] = total if i == 0 else out_ref[:, cols] + total
+            out_ref[:, cols] = total if pair == 0 else out_ref[:, cols] + total
+
+        @pl.loop(0, 3)
+        def _(j):
+            tile(pl.ds(pl.multiple_of(j * 256, 256), 256))
+
+        tile(pl.ds(768, 128))
 
     def place(zz):
         return (zz % 2) * 2 + zz // 2
@@ -272,21 +267,20 @@
             source = r_out
         for k in (1, 2, 3):
             zz = ring(zl, k)
-            copies.send(source.at[place(zz)], r_in.at[k - 1], r_sem.at[k - 1], dev(zl=zz))
+            copies.send(source.at[place(zz)], r_in.at[k - 1], r_sem.at[0], dev(zl=zz), shared=r_send_sem.at[0])
 
     def r_block(yy, zz):
         return rt.at[yy * 4 + zz]
 
-    def r_half(yy, zz, half):
-        return rt.at[yy * 4 + zz, pl.ds(half * 256, 256)]
+    def r_blocks(yy, first, count):
+        return rt.at[pl.ds(yy * 4 + first, count)]
 
     def send_r_y(zz):
-        copies.send(r_block(y, zz), r_block(y, zz), rt_y_sem.at[0, zz], up_y)
-        copies.send(r_block(y, zz), r_block(y, zz), rt_y_sem.at[1, zz], down_y)
+        copies.send(r_block(y, zz), r_block(y, zz), rt_y_sem.at[0], up_y, shared=rt_y_send_sem.at[0])
+        copies.send(r_block(y, zz), r_block(y, zz), rt_y_sem.at[1], down_y, shared=rt_y_send_sem.at[1])
 
     def sum_act():
-        for k in range(3):
-            got(r_in.at[k], r_sem.at[k])
+        got(r_in, r_sem.at[0])
         others = [r_in[k].astype(F32) for k in range(3)]
         own_r = (r_part[place(zl)] + others[0]) + (others[1] + others[2])
         rt[y * 4 + zl] = own_r.T.astype(BF16)
@@ -299,17 +293,23 @@
         got(r_block(y, zz), rt_z_sem.at[k - 1])
         send_r_y(zz)
 
-    def act_relay(k):
-        zz = ring(zl, -k)
-        got(r_block(low, zz), rt_y_sem.at[0, zz])
-        copies.send(r_half(low, zz, 0), r_half(low, zz, 0), rt_half_sem.at[0, zz], up_y)
-        got(r_block(high, zz), rt_y_sem.at[1, zz])
-        copies.send(r_half(high, zz, 1), r_half(high, zz, 1), rt_half_sem.at[1, zz], down_y)
+    def act_relay():
+        got(r_blocks(low, 0, 4), rt_y_sem.at[0])
+        copies.send(r_blocks(low, 0, 2), r_blocks(low, 0, 2), rt_half_sem.at[0], up_y)
+        got(r_blocks(high, 0, 4), rt_y_sem.at[1])
+        copies.send(r_blocks(high, 2, 2), r_blocks(high, 2, 2), rt_half_sem.at[1], down_y)
 
     def act_opposite():
-        for k in range(4):
-            got(r_half(opposite, k, 0), rt_half_sem.at[0, k])
-            got(r_half(opposite, k, 1), rt_half_sem.at[1, k])
+        got(r_blocks(opposite, 0, 2), rt_half_sem.at[0])
+        got(r_blocks(opposite, 2, 2), rt_half_sem.at[1])
+
+    def finish_shared():
+        for i in range(8):
+            got(x_in.at[i], x_send_sem.at[i])
+            got(grad.at[i, pl.ds(0, 96)], gx_send_sem.at[i])
+        got(r_in, r_send_sem.at[0])
+        for side in range(2):
+            got(r_blocks(y, 0, 4), rt_y_send_sem.at[side])
 
     def opposite_pair(h):
         for k in range(2):
@@ -322,7 +322,7 @@
         relay_shard_y(2 * far)
         relay_shard_y(2 * far + 1)
 
-    stages = [rotate, sum_core, sum_x, sum_z, spread_x, spread_core]
+    stages = [rotate, sum_core, sum_x, sum_z, spread_core]
 
     def slot(s):
         for stage in reversed(range(len(stages))):
@@ -335,8 +335,8 @@
     z_step(1)
     own_a.wait()
     slot(0)
+    z_step(2)
     tokens_core()
-    z_step(2)
     relay_shard_y(zl)
     rotate_act()
     z_step(3)
@@ -353,32 +353,27 @@
     act_y(3)
     opposite_pair(near)
     slot(6)
-    fit(0)
-    for k in range(4):
-        act_relay(k)
+    act_relay()
     opposite_pair(far)
     slot(7)
+    fit(0)
+    slot(8)
     fit(1)
-    slot(8)
+    slot(9)
     fit(2)
-    slot(9)
+    slot(10)
+    slot(11)
+    act_opposite()
     fit(3)
-    slot(10)
-    fit(4)
-    slot(11)
-    fit(5)
-    slot(12)
-    act_opposite()
-    fit(6)
-    fit(7)
+    finish_shared()
     copies.finish()
 
 
-def call(arrays, x_type, r_type, collective_id):
+def call(arrays, r_type, collective_id):
     vmem = pl.BlockSpec(memory_space=pltpu.VMEM)
     dma = pltpu.SemaphoreType.DMA
     return pl.pallas_call(
-        functools.partial(kernel, x_type, r_type),
+        functools.partial(kernel, r_type),
         out_shape=jax.ShapeDtypeStruct((512, 896), F32),
         in_specs=[vmem] * 4,
         out_specs=vmem,
@@ -386,10 +381,9 @@
             pltpu.VMEM((2048, 1792), BF16),
             pltpu.VMEM((8, 256, 896), F32),
             pltpu.VMEM((8, 128, 896), F32),
-            pltpu.VMEM((8, 4, 32, 896), BF16),
-            pltpu.VMEM((8, 3, 32, 896), x_type),
-            pltpu.VMEM((8, 2, 16, 896), F32),
-            pltpu.VMEM((8, 16, 896), F32),
+            pltpu.VMEM((8, 3, 32, 896), F32),
+            pltpu.VMEM((8, 32, 896), F32),
+            pltpu.VMEM((8, 32, 896), F32),
             pltpu.VMEM((8, 256, 896), BF16),
             pltpu.VMEM((2048, 512), BF16),
             pltpu.VMEM((2, 4, 2, 128, 512), BF16),
@@ -406,15 +400,18 @@
             dma((2, 2)),
             dma((4,)),
             dma((1,)),
+            dma((1,)),
+            dma((1,)),
             dma((3,)),
-            dma((3,)),
-            dma((2, 4)),
-            dma((2, 4)),
-            dma((8,)),
-            dma((8, 3)),
-            dma((8,)),
-            dma((8,)),
-            dma((8, 3)),
+            dma((2,)),
+            dma((2,)),
+            dma((2,)),
+            dma((8,)),
+            dma((8,)),
+            dma((8,)),
+            dma((8,)),
+            dma((8,)),
+            dma((8,)),
             dma((8,)),
         ],
         compiler_params=pltpu.CompilerParams(
@@ -429,6 +426,6 @@
     out_specs = P("tensor", "dp")
 
     def local(*arrays):
-        return call(arrays, F32, BF16, 0)
+        return call(arrays, BF16, 0)
 
     return jax.shard_map(local, mesh=mesh, in_specs=in_specs, out_specs=out_specs, check_vma=False)

time: 154 us -> 156 us (1.013)
  the two profiles are of different devices: /device:TPU:1 before, /device:TPU:65 now
where the time goes in v3:
time: 156 us
  Pallas kernels  153 us (98%)
  local copies, waits for them, and re-layouts  2.85 us (2%)
    pallas_call x1, Pallas kernels, call(): pl.pallas_call(functools.partial(kernel, r_type), out_shape=jax.ShapeDtyp...  153 us

profile of v3, /device:TPU:65, one launch (start us, length us, event | category | flops | bytes accessed | tf_op | source)
XLA Modules:
  0.0 155.7 jit_solution(6797197636615971144)
XLA Ops:
  0.0 152.9 %shard_map.46 = f32[512,896]{1,0:T(8,128)} custom-call(bf16[128,512]{1,0:T(8,128)(2,1)} %tokens_ref.1, bf16[128,1792]{1,0:T(8,128)(2,1)} %grads_ref.1, bf16[512,512]{1,0:T(8,128)(2,1)} %bin_ref.1, bf16[1792,896]{1,0:T(8,128)(2,1)} %bout_ref.1), custom_call_target="tpu_custom_call" | custom-call | flops 9600000000 | bytes 6000000 | tf_op jit(solution)/shard_map/pallas_call | solution.py:375
  152.9 2.8 %copy.6 = f32[512,896]{1,0:T(8,128)} copy(f32[512,896]{1,0:T(8,128)} %shard_map.46) | data formatting | bytes 3670016

commit v4 on v3

--- a/solution.py
+++ b/solution.py
@@ -334,35 +334,63 @@
     send_shard_y(zl, grads_ref)
     z_step(1)
     own_a.wait()
-    slot(0)
+    rotate(0)
+    sum_core(0)
     z_step(2)
     tokens_core()
     relay_shard_y(zl)
     rotate_act()
     z_step(3)
-    slot(1)
+    sum_x(0)
+    rotate(1)
     relay_shard_y(mate)
-    slot(2)
-    slot(3)
+    sum_core(1)
+    rotate(2)
+    rotate(3)
+    sum_z(0)
+    sum_core(2)
+    sum_core(3)
+    sum_x(1)
     sum_act()
     relay_far()
-    slot(4)
+    spread_core(0)
+    sum_z(1)
+    sum_x(2)
+    sum_x(3)
+    rotate(4)
+    rotate(5)
+    sum_core(4)
+    sum_core(5)
     act_y(1)
-    slot(5)
     act_y(2)
     act_y(3)
+    spread_core(1)
+    sum_z(2)
+    sum_z(3)
+    sum_x(4)
+    sum_x(5)
     opposite_pair(near)
-    slot(6)
+    rotate(6)
+    sum_core(6)
+    spread_core(2)
+    spread_core(3)
+    sum_z(4)
+    sum_z(5)
+    opposite_pair(far)
+    rotate(7)
+    sum_core(7)
     act_relay()
-    opposite_pair(far)
-    slot(7)
+    sum_x(6)
     fit(0)
-    slot(8)
+    spread_core(4)
+    spread_core(5)
+    sum_x(7)
+    sum_z(6)
     fit(1)
-    slot(9)
+    sum_z(7)
+    spread_core(6)
     fit(2)
-    slot(10)
-    slot(11)
+    spread_core(7)
     act_opposite()
     fit(3)
     finish_shared()

time: 156 us -> 149 us (0.955)
  the two profiles are of different devices: /device:TPU:65 before, /device:TPU:109 now
where the time goes in v4:
time: 149 us
  Pallas kernels  147 us (99%)
  local copies, waits for them, and re-layouts  2.85 us (2%)
    pallas_call x1, Pallas kernels, call(): pl.pallas_call(functools.partial(kernel, r_type), out_shape=jax.ShapeDtyp...  147 us

profile of v4, /device:TPU:109, one launch (start us, length us, event | category | flops | bytes accessed | tf_op | source)
XLA Modules:
  0.0 149.4 jit_solution(7599293422551882137)
XLA Ops:
  0.0 146.5 %shard_map.46 = f32[512,896]{1,0:T(8,128)} custom-call(bf16[128,512]{1,0:T(8,128)(2,1)} %tokens_ref.1, bf16[128,1792]{1,0:T(8,128)(2,1)} %grads_ref.1, bf16[512,512]{1,0:T(8,128)(2,1)} %bin_ref.1, bf16[1792,896]{1,0:T(8,128)(2,1)} %bout_ref.1), custom_call_target="tpu_custom_call" | custom-call | flops 9600000000 | bytes 6000000 | tf_op jit(solution)/shard_map/pallas_call | solution.py:403
  146.5 2.8 %copy.6 = f32[512,896]{1,0:T(8,128)} copy(f32[512,896]{1,0:T(8,128)} %shard_map.46) | data formatting | bytes 3670016

commit v5 on v4

--- a/solution.py
+++ b/solution.py
@@ -17,9 +17,10 @@
     def __init__(self, send_sems):
         self.send_sems = send_sems
         self.sent = []
+        self.count = 0
 
     def send(self, src, dst, recv_sem, to, cond=None, shared=None):
-        index = len(self.sent)
+        index = self.count
 
         def build():
             return pltpu.make_async_remote_copy(
@@ -36,10 +37,13 @@
         else:
             pl.when(cond)(lambda: build().start())
         if shared is None:
+            self.count += 1
             self.sent.append((build, cond))
 
-    def finish(self):
-        for build, cond in self.sent:
+    def finish(self, keep=0):
+        done = self.sent[:len(self.sent) - keep]
+        self.sent = self.sent[len(done):]
+        for build, cond in done:
             if cond is None:
                 build().wait_send()
             else:
@@ -48,9 +52,9 @@
 
 def kernel(
     r_type,
-    tokens_ref, grads_ref, bin_ref, bout_ref, out_ref,
+    tokens_ref, grads_ref, bin_ref, bout_hbm, out_ref,
     a_all, part, core_in, x_in, x_sum, z_in, grad, b1, a1, r_part, r_out, r_in, rt,
-    send_sems, local_sems, a_sem, a_half_sem, b1_sem, b1_half_sem, a1_first_sem, a1_x_sem, a1_core_sem,
+    bout_ref, send_sems, local_sems, a_sem, a_half_sem, b1_sem, b1_half_sem, a1_first_sem, a1_x_sem, a1_core_sem,
     r_sem, r_send_sem, rt_z_sem, rt_y_sem, rt_y_send_sem, rt_half_sem, core_sem, x_sem, x_send_sem, z_sem, gx_sem, gx_send_sem, gc_sem,
 ):
     dp, tensor = lax.axis_index("dp"), lax.axis_index("tensor")
@@ -67,6 +71,9 @@
     core_mate, z_mate = dev(c=1 - c), dev(zh=1 - zh)
     x_others = [dev(x=ring(x, k)) for k in (1, 2, 3)]
     copies = Copies(send_sems)
+
+    own_basis = pltpu.make_async_copy(bout_hbm, bout_ref, local_sems.at[3])
+    own_basis.start()
 
     barrier = pltpu.get_barrier_semaphore()
     greeted = 0
@@ -303,10 +310,15 @@
         got(r_blocks(opposite, 0, 2), rt_half_sem.at[0])
         got(r_blocks(opposite, 2, 2), rt_half_sem.at[1])
 
-    def finish_shared():
+    def finish_sums():
         for i in range(8):
             got(x_in.at[i], x_send_sem.at[i])
+
+    def finish_spreads(first, last):
+        for i in range(first, last):
             got(grad.at[i, pl.ds(0, 96)], gx_send_sem.at[i])
+
+    def finish_act():
         got(r_in, r_send_sem.at[0])
         for side in range(2):
             got(r_blocks(y, 0, 4), rt_y_send_sem.at[side])
@@ -334,66 +346,72 @@
     send_shard_y(zl, grads_ref)
     z_step(1)
     own_a.wait()
+    own_basis.wait()
     rotate(0)
     sum_core(0)
     z_step(2)
     tokens_core()
     relay_shard_y(zl)
+    sum_x(0)
     rotate_act()
     z_step(3)
-    sum_x(0)
     rotate(1)
     relay_shard_y(mate)
     sum_core(1)
     rotate(2)
     rotate(3)
-    sum_z(0)
     sum_core(2)
     sum_core(3)
+    sum_z(0)
     sum_x(1)
     sum_act()
     relay_far()
-    spread_core(0)
-    sum_z(1)
-    sum_x(2)
-    sum_x(3)
     rotate(4)
     rotate(5)
+    spread_core(0)
     sum_core(4)
     sum_core(5)
+    sum_x(2)
+    sum_z(1)
+    sum_x(3)
     act_y(1)
+    opposite_pair(near)
+    rotate(6)
     act_y(2)
     act_y(3)
-    spread_core(1)
+    sum_core(6)
     sum_z(2)
     sum_z(3)
+    spread_core(1)
     sum_x(4)
     sum_x(5)
-    opposite_pair(near)
-    rotate(6)
-    sum_core(6)
+    opposite_pair(far)
+    rotate(7)
     spread_core(2)
     spread_core(3)
+    sum_core(7)
+    act_relay()
     sum_z(4)
     sum_z(5)
-    opposite_pair(far)
-    rotate(7)
-    sum_core(7)
-    act_relay()
     sum_x(6)
     fit(0)
+    copies.finish(25)
+    sum_x(7)
+    sum_z(6)
     spread_core(4)
     spread_core(5)
-    sum_x(7)
-    sum_z(6)
     fit(1)
+    finish_sums()
     sum_z(7)
     spread_core(6)
     fit(2)
+    finish_spreads(0, 6)
+    finish_act()
     spread_core(7)
+    copies.finish(3)
+    finish_spreads(6, 8)
     act_opposite()
     fit(3)
-    finish_shared()
     copies.finish()
 
 
@@ -403,7 +421,7 @@
     return pl.pallas_call(
         functools.partial(kernel, r_type),
         out_shape=jax.ShapeDtypeStruct((512, 896), F32),
-        in_specs=[vmem] * 4,
+        in_specs=[vmem] * 3 + [pl.BlockSpec(memory_space=pl.ANY)],
         out_specs=vmem,
         scratch_shapes=[
             pltpu.VMEM((2048, 1792), BF16),
@@ -419,8 +437,9 @@
             pltpu.VMEM((4, 128, 512), BF16),
             pltpu.VMEM((3, 128, 512), r_type),
             pltpu.VMEM((16, 512, 128), BF16),
+            pltpu.VMEM((1792, 896), BF16),
             dma((200,)),
-            dma((3,)),
+            dma((4,)),
             dma((3, 4)),
             dma((2, 4)),
             dma((2,)),

time: 149 us -> 151 us (1.013)
  the two profiles are of different devices: /device:TPU:109 before, /device:TPU:113 now
where the time goes in v5:
time: 151 us
  Pallas kernels  148 us (98%)
  local copies, waits for them, and re-layouts  2.85 us (2%)
    pallas_call x1, Pallas kernels, call(): pl.pallas_call(functools.partial(kernel, r_type), out_shape=jax.ShapeDtyp...  148 us

profile of v5, /device:TPU:113, one launch (start us, length us, event | category | flops | bytes accessed | tf_op | source)
XLA Modules:
  0.0 150.5 jit_solution(12329741819833435100)
XLA Ops:
  0.0 147.7 %shard_map.46 = f32[512,896]{1,0:T(8,128)} custom-call(bf16[128,512]{1,0:T(8,128)(2,1)} %tokens_ref.1, bf16[128,1792]{1,0:T(8,128)(2,1)} %grads_ref.1, bf16[512,512]{1,0:T(8,128)(2,1)} %bin_ref.1, bf16[1792,896]{1,0:T(8,128)(2,1)} %bout_hbm.1), custom_call_target="tpu_custom_call" | custom-call | flops 9600000000 | bytes 6000000 | tf_op jit(solution)/shard_map/pallas_call | solution.py:421
  147.7 2.8 %copy.6 = f32[512,896]{1,0:T(8,128)} copy(f32[512,896]{1,0:T(8,128)} %shard_map.46) | data formatting | bytes 3670016

commit v6 on v5

--- a/solution.py
+++ b/solution.py
@@ -331,8 +331,8 @@
     mate = zl + 1 - 2 * (zl % 2)
 
     def relay_far():
-        relay_shard_y(2 * far)
-        relay_shard_y(2 * far + 1)
+        relay_shard_y(1 + far)
+        relay_shard_y(3 * far)
 
     stages = [rotate, sum_core, sum_x, sum_z, spread_core]
 

time: 151 us -> 151 us (level)
  no operation moved by 1% of the time
where the time goes in v6:
time: 151 us
  Pallas kernels  148 us (98%)
  local copies, waits for them, and re-layouts  2.85 us (2%)
    pallas_call x1, Pallas kernels, call(): pl.pallas_call(functools.partial(kernel, r_type), out_shape=jax.ShapeDtyp...  148 us

profile of v6, /device:TPU:113, one launch (start us, length us, event | category | flops | bytes accessed | tf_op | source)
XLA Modules:
  0.0 150.5 jit_solution(12089968792840885670)
XLA Ops:
  0.0 147.7 %shard_map.46 = f32[512,896]{1,0:T(8,128)} custom-call(bf16[128,512]{1,0:T(8,128)(2,1)} %tokens_ref.1, bf16[128,1792]{1,0:T(8,128)(2,1)} %grads_ref.1, bf16[512,512]{1,0:T(8,128)(2,1)} %bin_ref.1, bf16[1792,896]{1,0:T(8,128)(2,1)} %bout_hbm.1), custom_call_target="tpu_custom_call" | custom-call | flops 9600000000 | bytes 6000000 | tf_op jit(solution)/shard_map/pallas_call | solution.py:421
  147.7 2.8 %copy.6 = f32[512,896]{1,0:T(8,128)} copy(f32[512,896]{1,0:T(8,128)} %shard_map.46) | data formatting | bytes 3670016

commit v7 on v6

--- a/solution.py
+++ b/solution.py
@@ -245,6 +245,16 @@
 
         tile(pl.ds(768, 128))
 
+    def mirror(v):
+        return jnp.where(zl < 2, v, 3 - v)
+
+    last = mirror(1 - jnp.minimum(zl, 3 - zl))
+    far_first = [mirror(3), mirror(2), last]
+    arrivals = [mirror(2), mirror(3), last]
+
+    def gap(source, target):
+        return lax.rem(target - source + 4, 4) - 1
+
     def place(zz):
         return (zz % 2) * 2 + zz // 2
 
@@ -272,9 +282,8 @@
         if r_type != F32:
             r_out[...] = r_part[...].astype(r_type)
             source = r_out
-        for k in (1, 2, 3):
-            zz = ring(zl, k)
-            copies.send(source.at[place(zz)], r_in.at[k - 1], r_sem.at[0], dev(zl=zz), shared=r_send_sem.at[0])
+        for zz in far_first:
+            copies.send(source.at[place(zz)], r_in.at[gap(zl, zz)], r_sem.at[0], dev(zl=zz), shared=r_send_sem.at[0])
 
     def r_block(yy, zz):
         return rt.at[yy * 4 + zz]
@@ -291,13 +300,13 @@
         others = [r_in[k].astype(F32) for k in range(3)]
         own_r = (r_part[place(zl)] + others[0]) + (others[1] + others[2])
         rt[y * 4 + zl] = own_r.T.astype(BF16)
-        for k in (1, 2, 3):
-            copies.send(r_block(y, zl), r_block(y, zl), rt_z_sem.at[k - 1], dev(zl=ring(zl, k)))
+        for zz in far_first:
+            copies.send(r_block(y, zl), r_block(y, zl), rt_z_sem.at[gap(zl, zz)], dev(zl=zz))
         send_r_y(zl)
 
     def act_y(k):
-        zz = ring(zl, -k)
-        got(r_block(y, zz), rt_z_sem.at[k - 1])
+        zz = arrivals[k - 1]
+        got(r_block(y, zz), rt_z_sem.at[gap(zz, zl)])
         send_r_y(zz)
 
     def act_relay():

time: 151 us -> 146 us (0.967)
  the two profiles are of different devices: /device:TPU:113 before, /device:TPU:89 now
where the time goes in v7:
time: 146 us
  Pallas kernels  143 us (98%)
  local copies, waits for them, and re-layouts  2.85 us (2%)
    pallas_call x1, Pallas kernels, call(): pl.pallas_call(functools.partial(kernel, r_type), out_shape=jax.ShapeDtyp...  143 us

profile of v7, /device:TPU:89, one launch (start us, length us, event | category | flops | bytes accessed | tf_op | source)
XLA Modules:
  0.0 145.9 jit_solution(16521053986074844238)
XLA Ops:
  0.0 143.0 %shard_map.46 = f32[512,896]{1,0:T(8,128)} custom-call(bf16[128,512]{1,0:T(8,128)(2,1)} %tokens_ref.1, bf16[128,1792]{1,0:T(8,128)(2,1)} %grads_ref.1, bf16[512,512]{1,0:T(8,128)(2,1)} %bin_ref.1, bf16[1792,896]{1,0:T(8,128)(2,1)} %bout_hbm.1), custom_call_target="tpu_custom_call" | custom-call | flops 9600000000 | bytes 6000000 | tf_op jit(solution)/shard_map/pallas_call | solution.py:430
  143.0 2.8 %copy.6 = f32[512,896]{1,0:T(8,128)} copy(f32[512,896]{1,0:T(8,128)} %shard_map.46) | data formatting | bytes 3670016
